TPU v7x, 512 devices: a whole 4x4x16 slice. The times are simulated.
512 devices in a mesh: dp: 64 (over z, x_hi, core), param: 8 (over x_lo, y).
Axes of the slice: x: 4 (x_hi: 2, x_lo: 2; x = x_hi * 2 + x_lo), y: 4, z: 16, core: 2. Of those that a mesh axis runs over, the one named last changes fastest.
Arguments:
- output_gradient: bfloat16 [65536, 4096], P('dp', 'param'), may hold values from -6 to 6
- adapter_activations: bfloat16 [65536, 64], P('dp'), may hold values from -6 to 6
- proj: bfloat16 [4096, 64, 4096], P(('param', 'dp')), may hold values from -0.01171875 to 0.01171875
- labels: int32 [256], P('dp'), may hold values from 0 to 31
Outputs:
- scores: float32 [256, 32], P('dp')
- task_means: float32 [32, 4096], P(None, 'param')
All inputs are finite; a program needn't handle non-finite values.
Results may differ from a plain program's by a relative error of at most 0.0029.
Values may be sent and summed in bfloat16 or wider, within the bound.
A program may use at most 64 MiB of HBM per device.

v0:
```python
import jax
import jax.numpy as jnp
from jax import lax
from jax.sharding import PartitionSpec as P

K = 4096
NT = 32


epsilon = 1e-06


def body(output_gradient, adapter_activations, proj, labels):
    local_examples = labels.shape[0]
    token_rows = output_gradient.shape[0] // local_examples
    grad_tok = output_gradient.reshape(local_examples, token_rows, output_gradient.shape[1])
    activation_tokens = adapter_activations.reshape(
        local_examples, token_rows, adapter_activations.shape[1]
    )
    gradient = jnp.einsum(
        "eto,etr->eor", grad_tok, activation_tokens, preferred_element_type=jnp.float32
    ).astype(jnp.bfloat16)
    pieces = lax.all_to_all(gradient, "dp", split_axis=1, concat_axis=0, tiled=True)
    pool_size = pieces.shape[0]
    flat_rows = pieces.reshape(pool_size, pieces.shape[1] * pieces.shape[2])
    proj_rows = proj.reshape(proj.shape[0] * proj.shape[1], proj.shape[2])
    mine = lax.psum_scatter(
        jnp.dot(flat_rows, proj_rows, preferred_element_type=jnp.float32),
        "dp",
        scatter_dimension=0,
        tiled=True,
    )
    projected = lax.psum_scatter(mine, "param", scatter_dimension=1, tiled=True)
    onehot = (labels[:, None] == jnp.arange(NT, dtype=jnp.int32)[None, :]).astype(jnp.float32)
    totals = jnp.dot(onehot.T, projected, precision=lax.Precision.HIGHEST)
    counts = jnp.sum(onehot, axis=0)
    totals, counts = lax.psum((totals, counts), "dp")
    task_means = totals / jnp.maximum(counts, 1.0)[:, None]
    score_dots = jnp.dot(projected, task_means.T, precision=lax.Precision.HIGHEST)
    grad_sq = jnp.sum(projected * projected, axis=1)
    mean_sq = jnp.sum(task_means * task_means, axis=1)
    score_dots, grad_sq, mean_sq = lax.psum((score_dots, grad_sq, mean_sq), "param")
    scores = (
        score_dots
        / K
        * lax.rsqrt(grad_sq / K + epsilon)[:, None]
        * lax.rsqrt(mean_sq / K + epsilon)[None, :]
    )
    return (scores, task_means)


def solution(mesh):
    placed = (P("dp", "param"), P("dp", None), P(("param", "dp"), None, None), P("dp"))
    return jax.shard_map(
        body,
        mesh=mesh,
        in_specs=placed,
        out_specs=(P("dp", None), P(None, "param")),
        check_vma=False,
    )
```

profile of v0, /device:TPU:1, one launch (start us, length us, event | category | flops | bytes accessed | tf_op | source)
XLA Modules:
  0.0 1119.8 jit_solution(13843757269088088392)
XLA Ops:
  7.2 1.2 copy-done
  8.4 1.2 convolution_convert_fusion
  9.6 0.3 copy.15
  9.9 0.3 reshape.28
  10.2 43.2 %all_to_all.15 = bf16[64,2,1024]{2,1,0:T(2,128)(2,1)S(1)} all-to-all(bf16[64,2,1024]{2,1,0:T(2,128)(2,1)S(1)} %reshape.28), channel_id=1, replica_groups=mesh['dp'=64,'param'=8] {'dp'}, dimensions={0} | all-to-all | bytes 524288 | tf_op jit(solution)/shard_map/all_to_all | solution.py:23
  53.4 0.3 reshape.29
  53.9 0.1 copy.17
  54.0 0.3 reshape.23
  54.3 5.4 fusion.7
  59.8 1.3 dynamic-slice
  61.7 0.1 convert_reduce_fusion
  61.8 127.9 %psum.36 = f32[32]{0:T(128)S(1)} all-reduce(f32[32]{0:T(128)S(1)} %convert_reduce_fusion), channel_id=1, replica_groups=mesh['dp'=64,'param'=8] {'dp'}, use_global_device_ids=true, to_apply=%region_4.0 | all-reduce | flops 32 | bytes 256 | tf_op jit(solution)/shard_map/psum | solution.py:37
  189.7 399.3 %all-reduce.7.cloned.1.call-done = f32[256,4096]{1,0:T(8,128)} async-done(((f32[256,4096]{1,0:T(8,128)}), f32[256,4096]{1,0:T(8,128)}) %all-reduce.7.cloned.1.call-update) | async-done | bytes 4194320
  589.0 0.9 constant_dynamic-slice_fusion
  589.9 2.0 copy.18
  592.0 44.3 %reduce-scatter.4.cloned.1.call-done = f32[512,4]{1,0:T(8,128)} async-done(((f32[4096,4]{1,0:T(8,128)}), f32[512,4]{1,0:T(8,128)}) %reduce-scatter.4.cloned.1.call-update) | async-done | bytes 8208
  636.3 1.9 fusion.2
  638.3 1.1 copy.19
  639.3 0.1 multiply_reduce_fusion.1
  639.4 455.6 %all-reduce.5.cloned.1.call-done = f32[32,512]{1,0:T(8,128)} async-done(((f32[32,512]{1,0:T(8,128)}), f32[32,512]{1,0:T(8,128)}) %all-reduce.5.cloned.1.call-update) | async-done | bytes 65552 | tf_op jit(solution)/shard_map/psum | solution.py:37
  1095.0 1.0 multiply_reduce_fusion
  1096.1 1.5 fusion.4
  1097.6 15.0 %all-reduce.1 = (f32[4,32]{1,0:T(4,128)S(1)}, f32[32]{0:T(128)S(1)}, f32[4]{0:T(128)S(1)}) all-reduce(f32[4,32]{1,0:T(4,128)S(1)} %fusion.4, f32[32]{0:T(128)S(1)} %get-tuple-element.5, f32[4]{0:T(128)S(1)} %multiply_reduce_fusion.1), channel_id=1, replica_groups=mesh['dp'=64,'param'=8] {'param'}, use_global_device_ids=true, to_apply=%region_5.0 | all-reduce | flops 164 | bytes 1312 | tf_op jit(solution)/shard_map/psum | solution.py:42
  1112.6 0.7 multiply_multiply_fusion
  (15 shorter events, 0.3 us)
Async XLA Ops:
  7.2 1.2 copy-start
  7.2 581.8 %all-reduce.7.cloned.1.call-start = ((), (), s32[]{:S(2)}) async-start(), calls=%async_computation.4 | async-start | bytes 8388608
  59.7 2.0 copy-start.2
  59.7 576.6 %reduce-scatter.4.cloned.1.call-start = ((), (), s32[]{:S(2)}) async-start(), calls=%async_computation.3 | async-start | bytes 2359296
  591.9 503.1 %all-reduce.5.cloned.1.call-start = ((), (), s32[]{:S(2)}) async-start(), calls=%async_computation.2 | async-start | bytes 131072 | tf_op jit(solution)/shard_map/psum | solution.py:37
  1096.1 17.2 %copy-start.1 = (f32[32,512]{1,0:T(8,128)}, f32[32,512]{1,0:T(8,128)S(1)}, u32[]{:S(2)}) copy-start(f32[32,512]{1,0:T(8,128)S(1)} %get-tuple-element.6) | copy-start | bytes 196612
Sparse Core Ops, SparseCore 0:
  59.8 529.0 all-reduce.6
  592.1 44.1 reduce-scatter.3
  640.0 454.9 all-reduce.4
where the time goes:
time: 1120 us
  waiting for transfers between devices  899 us (80%)
  blocking collectives  186 us (17%)
  between operations  14.5 us (1%)
    psum x1, waiting for transfers between devices, body(): totals, counts = lax.psum((totals, counts), 'dp')  456 us
    unnamed x5, waiting for transfers between devices  444 us
    psum x1, blocking collectives, body(): totals, counts = lax.psum((totals, counts), 'dp')  128 us
    all_to_all x1, blocking collectives, body(): lax.all_to_all(gradient, 'dp', split_axis=1, concat_axis=0, tiled=True)  43.2 us
  transfers between devices with their start and end apart: 3, of which 3 were waited for; matrix products, arithmetic and copies ran while one was open for 0% of the time, Pallas kernels for 0%

commit v1 on v0

v1 whole, which is shorter than its diff:
```python
import functools

import jax
import jax.numpy as jnp
from jax import lax
from jax.experimental import pallas as pl
from jax.experimental.pallas import tpu as pltpu
from jax.sharding import PartitionSpec as P

K = 4096
NT = 32
EPSILON = 1e-06
MESH = pl.DeviceIdType.MESH
F32 = jnp.float32
BF16 = jnp.bfloat16
HIGHEST = lax.Precision.HIGHEST

OFFSETS = (0, 8, 1, 15, 7, 9, 2, 14, 6, 10, 3, 13, 5, 11, 4, 12)
GROUPS = 4


def kernel(
    og_h, act_h, proj_h, lab_ref, scores_ref, means_ref,
    og_v, act_v, proj_v, g32, s32, qs, rq, rb, f32s, ls, lr,
    own, cs, cr, ao, bo, sa, ra, sb, rbb, sa2, ra2, sb2, rb2,
    dsum, zs32, zs, zr, tsum, zts, ztr, qas, qar, agr, pks, pkr,
    in_sem, loc_sem, lab_sem, quad_sem, zg_send, zg_recv, core_sem,
    xa_sem, yb_sem, ya_sem, xb_sem, zs_send, zs_recv, zt_sem, qa_sem, ag_sem, pk_sem,
):
    nz = 16
    per = nz // GROUPS
    rw = per * 4
    dp, param = lax.axis_index("dp"), lax.axis_index("param")
    z, q = dp // 4, dp % 4
    xl, y = param // 4, param % 4

    def xor(value, bits):
        out = value
        if bits & 1:
            out = out + 1 - 2 * (value % 2)
        if bits & 2:
            out = out + 2 - 4 * ((value // 2) % 2)
        if bits & 4:
            out = out + 4 - 8 * ((value // 4) % 2)
        return out

    def ahead(i):
        return ((z + OFFSETS[i]) % nz) * 4 + q

    def behind(i):
        return ((z + nz - OFFSETS[i]) % nz) * 4 + q

    def x_peer(a):
        return (xor(dp, a & 2), xor(param, (a & 1) * 4))

    def y_peer(r):
        return (dp, xor(param, r))

    def remote(src, dst, send, recv, device):
        return pltpu.make_async_remote_copy(
            src_ref=src, dst_ref=dst, send_sem=send, recv_sem=recv,
            device_id=device, device_id_type=MESH,
        )

    def wait_all(ref, sem):
        pltpu.make_async_copy(ref, ref, sem).wait()

    barrier = pltpu.get_barrier_semaphore()
    peers = [(xor(dp, s), param) for s in (1, 2, 3)]
    peers += [(ahead(i), param) for i in range(1, nz)]
    peers += [(dp, xor(param, r)) for r in range(1, 8)]
    peers += [x_peer(3)]
    for peer in peers:
        pl.semaphore_signal(barrier, inc=1, device_id=peer, device_id_type=MESH)

    act_in = pltpu.make_async_copy(act_h, act_v, in_sem.at[0])
    act_in.start()
    og_in = []
    for m in range(4):
        copy = pltpu.make_async_copy(
            og_h.at[pl.ds(m * 256, 256)], og_v.at[pl.ds(m * 256, 256)], in_sem.at[2 + m]
        )
        copy.start()
        og_in.append(copy)
    proj_in = pltpu.make_async_copy(proj_h, proj_v, in_sem.at[1])
    proj_in.start()

    lane = lax.broadcasted_iota(jnp.int32, (1, 128), 1)
    label_row = jnp.zeros((1, 128), jnp.int32)
    for m in range(4):
        label_row = jnp.where(lane % 4 == m, lab_ref[0:1, m : m + 1], label_row)
    ls[...] = label_row

    act_in.wait()
    low = lax.broadcasted_iota(jnp.int32, (64, 128), 1) < 64
    for m in range(4):
        og_in[m].wait()
        act = act_v[m * 256 : (m + 1) * 256, :]
        g32[m] = lax.dot_general(
            og_v[m * 256 : (m + 1) * 256, :],
            jnp.concatenate([act, act], axis=1),
            (((0,), (0,)), ((), ())),
            preferred_element_type=F32,
        )
        for j in range(4):
            even = g32[m, pl.ds(2 * j, 64, stride=8), :]
            odd = g32[m, pl.ds(2 * j + 1, 64, stride=8), :]
            s32[pl.ds(m * 4 + j, 64, stride=16), :] = jnp.where(low, even, odd)
    for block in range(nz):
        qs[block] = s32[block * 64 : (block + 1) * 64, :].astype(BF16).reshape(4, 16, 128)

    pl.semaphore_wait(barrier, len(peers))

    quad = []
    for s in (1, 2, 3):
        copy = remote(
            qs.at[:, xor(q, s)], rq.at[:, s], quad_sem.at[0, s], quad_sem.at[1, s], (xor(dp, s), param)
        )
        copy.start()
        quad.append(copy)
    mine = pltpu.make_async_copy(qs.at[:, q], rq.at[:, 0], loc_sem.at[0])
    mine.start()
    labels = []
    for i in range(1, nz):
        copy = remote(ls, lr.at[i], lab_sem.at[0], lab_sem.at[1], (ahead(i), param))
        copy.start()
    lr[0] = label_row
    mine.wait()
    for copy in quad:
        copy.wait()

    home = pltpu.make_async_copy(rq.at[z], rb.at[0], loc_sem.at[1])
    home.start()
    for i in range(1, nz):
        remote(
            rq.at[ahead(i) // 4], rb.at[i], zg_send, zg_recv.at[i // per], (ahead(i), param)
        ).start()
    home.wait()
    proj_in.wait()

    def project(c):
        first = max(1, c * per)
        wait_all(rb.at[pl.ds(first, (c + 1) * per - first)], zg_recv.at[c])
        for s in range(4):
            for k in range(per):
                at = (s * per + k) * 16
                f32s[c, at : at + 16, :] = rb[c * per + k, s].astype(F32)
        rows = jnp.concatenate(
            [f32s[c, pl.ds(j, 4 * rw, stride=4), :].astype(BF16) for j in range(4)], axis=1
        )
        for x in range(2):
            for r in range(4):
                column = xor(xl, x) * 4 + xor(y, r)
                part = jnp.dot(
                    rows,
                    proj_v[:, pl.ds(pl.multiple_of(column * 512, 512), 512)],
                    preferred_element_type=F32,
                )
                for h in range(2):
                    own[c, h * 2 + x, r] = part[2 * h * rw : (2 * h + 1) * rw]
                    cs[c, h * 2 + x, r] = part[(2 * h + 1) * rw : (2 * h + 2) * rw].astype(BF16)
        remote(
            cs.at[c], cr.at[c], core_sem.at[0, c], core_sem.at[1, c], (xor(dp, 1), param)
        ).start()

    def after_core(c):
        wait_all(cr.at[c], core_sem.at[1, c])
        for a in range(4):
            for r in range(4):
                total = own[c, a, r] + cr[c, a, r].astype(F32)
                if a == 0:
                    ao[c, r] = total[:, :256]
                else:
                    sa[c, a - 1, r] = total[:, :256].astype(BF16)
                if r == 0:
                    bo[c, a] = total[:, 256:]
                else:
                    sb[c, r - 1, a] = total[:, 256:].astype(BF16)
        for n in (1, 2, 3):
            remote(sa.at[c, n - 1], ra.at[c, n - 1], xa_sem.at[0, c], xa_sem.at[1, c], x_peer(n)).start()
            remote(sb.at[c, n - 1], rbb.at[c, n - 1], yb_sem.at[0, c], yb_sem.at[1, c], y_peer(n)).start()

    def after_first(c):
        wait_all(ra.at[c], xa_sem.at[1, c])
        for r in (1, 2, 3, 0):
            total = ao[c, r]
            for n in range(3):
                total += ra[c, n, r].astype(F32)
            if r == 0:
                ao[c, 0] = total
            else:
                sa2[c, r - 1] = total
        for n in (1, 2, 3):
            remote(sa2.at[c, n - 1], ra2.at[c, n - 1], ya_sem.at[0, c], ya_sem.at[1, c], y_peer(n)).start()
        wait_all(rbb.at[c], yb_sem.at[1, c])
        for a in (1, 2, 3, 0):
            total = bo[c, a]
            for n in range(3):
                total += rbb[c, n, a].astype(F32)
            if a == 0:
                bo[c, 0] = total
            else:
                sb2[c, a - 1] = total
        for n in (1, 2, 3):
            remote(sb2.at[c, n - 1], rb2.at[c, n - 1], xb_sem.at[0, c], xb_sem.at[1, c], x_peer(n)).start()

    def after_second(c):
        wait_all(ra2.at[c], ya_sem.at[1, c])
        total = ao[c, 0] + ra2[c, 0] + ra2[c, 1] + ra2[c, 2]
        dsum[0, c * rw : (c + 1) * rw, :] = total[:, :128]
        dsum[1, c * rw : (c + 1) * rw, :] = total[:, 128:]
        wait_all(rb2.at[c], xb_sem.at[1, c])
        total = bo[c, 0] + rb2[c, 0] + rb2[c, 1] + rb2[c, 2]
        dsum[2, c * rw : (c + 1) * rw, :] = total[:, :128]
        dsum[3, c * rw : (c + 1) * rw, :] = total[:, 128:]

    def send_examples(c):
        base = c * per * 16
        for j in range(4):
            for m in range(4):
                zs32[pl.ds(base + j * 4 + m, per, stride=16), :] = dsum[
                    j, pl.ds(c * rw + m, per, stride=4), :
                ]
        for k in range(per):
            i = c * per + k
            zs[i] = zs32[i * 16 : (i + 1) * 16, :].astype(BF16)
        for i in range(max(1, c * per), (c + 1) * per):
            remote(zs.at[i], zr.at[i], zs_send, zs_recv, (behind(i), param)).start()

    for step in range(GROUPS + 2):
        if 0 <= step - 3 < GROUPS:
            after_second(step - 3)
            send_examples(step - 3)
        if 0 <= step - 2 < GROUPS:
            after_first(step - 2)
        if 0 <= step - 1 < GROUPS:
            after_core(step - 1)
        if step < GROUPS:
            project(step)
    after_second(GROUPS - 1)

    wait_all(lr.at[pl.ds(1, nz - 1)], lab_sem.at[1])
    all_labels = jnp.zeros((1, 128), jnp.int32)
    for i in range(nz):
        all_labels = jnp.where(lane // 4 == i, lr[i], all_labels)
    all_labels = jnp.where(lane < 4 * nz, all_labels, -1)
    row = lax.broadcasted_iota(jnp.int32, (NT, 4 * nz), 0)
    tag = row % 2
    for i in range(nz):
        tag = jnp.where(row // 2 == i, row % 2 + 2 * (behind(i) // 4), tag)
    onehot = (tag == all_labels[:, : 4 * nz]).astype(F32)
    for j in range(4):
        tsum[j] = jnp.dot(onehot, dsum[j], precision=HIGHEST, preferred_element_type=F32)
        for t in range(2):
            zts[pl.ds(2 * j + t, nz, stride=8), :] = tsum[j, pl.ds(t, nz, stride=2), :]
    for i in range(1, nz):
        remote(zts.at[pl.ds(i * 8, 8)], ztr.at[i], zt_sem.at[0], zt_sem.at[1], (behind(i), param)).start()
    send_examples(GROUPS - 1)

    pair = lax.broadcasted_iota(jnp.int32, (8, 128), 0) % 2 + 2 * z
    counts = jnp.sum((pair == all_labels).astype(F32), axis=1, keepdims=True)
    wait_all(ztr.at[pl.ds(1, nz - 1)], zt_sem.at[1])
    pair_total = zts[0:8, :]
    for i in range(1, nz):
        pair_total += ztr[i]
    qas[0] = pair_total
    qas[1] = jnp.broadcast_to(counts, (8, 128))
    for s in (1, 2, 3):
        remote(qas, qar.at[s - 1], qa_sem.at[0], qa_sem.at[1], (xor(dp, s), param)).start()
    wait_all(qar, qa_sem.at[1])
    pair_total = qas[0] + qar[0, 0] + qar[1, 0] + qar[2, 0]
    pair_count = qas[1] + qar[0, 1] + qar[1, 1] + qar[2, 1]
    mine8 = pl.multiple_of(z * 8, 8)
    agr[pl.ds(mine8, 8), :] = pair_total / jnp.maximum(pair_count, 1.0)
    for i in range(1, nz):
        remote(
            agr.at[pl.ds(mine8, 8)], agr.at[pl.ds(mine8, 8)], ag_sem.at[0], ag_sem.at[1], (ahead(i), param)
        ).start()

    wait_all(zr.at[pl.ds(1, nz - 1)], zs_recv)
    mine16 = zs32[0:16, :]
    for i in range(1, nz):
        mine16 += zr[i].astype(F32)

    wait_all(agr.at[pl.ds(0, (nz - 1) * 8)], ag_sem.at[1])
    dots = jnp.zeros((4, NT), F32)
    mean_sq = jnp.zeros((4, NT), F32)
    grad_sq = jnp.zeros((4, 128), F32)
    ones = jnp.ones((4, 128), F32)
    contract = (((1,), (1,)), ((), ()))
    for j in range(4):
        for t in range(2):
            tsum[j, pl.ds(t, nz, stride=2), :] = agr[pl.ds(2 * j + t, nz, stride=8), :]
        means = tsum[j]
        means_ref[:, j * 128 : (j + 1) * 128] = means
        part = mine16[j * 4 : (j + 1) * 4, :]
        dots += lax.dot_general(part, means, contract, precision=HIGHEST, preferred_element_type=F32)
        mean_sq += lax.dot_general(ones, means * means, contract, precision=HIGHEST, preferred_element_type=F32)
        grad_sq += part * part
    grad_sq = jnp.sum(grad_sq, axis=1, keepdims=True)
    pks[...] = jnp.zeros((8, 128), F32)
    pks[0:4, 0:NT] = dots
    pks[4:8, 0:NT] = mean_sq
    pks[0:4, 64:128] = jnp.broadcast_to(grad_sq, (4, 64))
    for n in range(1, 8):
        remote(pks, pkr.at[n - 1], pk_sem.at[0], pk_sem.at[1], (dp, xor(param, n))).start()
    wait_all(rb.at[pl.ds(1, nz - 1)], zg_send)
    wait_all(lr.at[pl.ds(1, nz - 1)], lab_sem.at[0])
    for c in range(GROUPS):
        wait_all(cs.at[c], core_sem.at[0, c])
        wait_all(sa.at[c], xa_sem.at[0, c])
        wait_all(sb.at[c], yb_sem.at[0, c])
        wait_all(sa2.at[c], ya_sem.at[0, c])
        wait_all(sb2.at[c], xb_sem.at[0, c])
    wait_all(zs.at[pl.ds(1, nz - 1)], zs_send)
    wait_all(ztr.at[pl.ds(1, nz - 1)], zt_sem.at[0])
    wait_all(qar, qa_sem.at[0])
    wait_all(agr.at[pl.ds(0, (nz - 1) * 8)], ag_sem.at[0])
    wait_all(pkr, pk_sem.at[1])
    total = pks[...]
    for n in range(7):
        total += pkr[n]
    scores_ref[...] = (
        total[0:4, 0:NT]
        / K
        * lax.rsqrt(total[0:4, 64 : 64 + NT] / K + EPSILON)
        * lax.rsqrt(total[4:8, 0:NT] / K + EPSILON)
    )
    wait_all(pkr, pk_sem.at[0])


def body(output_gradient, adapter_activations, proj, labels):
    nz, g = 16, GROUPS
    per = nz // g
    rw = per * 4
    proj = proj.reshape(proj.shape[0] * proj.shape[1], proj.shape[2])
    vm = pltpu.VMEM
    scratch = [
        vm((1024, 512), BF16),
        vm((1024, 64), BF16),
        vm((512, K), BF16),
        vm((4, 512, 128), F32),
        vm((1024, 128), F32),
        vm((nz, 4, 16, 128), BF16),
        vm((nz, 4, 16, 128), BF16),
        vm((nz, 4, 16, 128), BF16),
        vm((g, per * 64, 128), F32),
        vm((1, 128), jnp.int32),
        vm((nz, 1, 128), jnp.int32),
        vm((g, 4, 4, rw, 512), F32),
        vm((g, 4, 4, rw, 512), BF16),
        vm((g, 4, 4, rw, 512), BF16),
        vm((g, 4, rw, 256), F32),
        vm((g, 4, rw, 256), F32),
        vm((g, 3, 4, rw, 256), BF16),
        vm((g, 3, 4, rw, 256), BF16),
        vm((g, 3, 4, rw, 256), BF16),
        vm((g, 3, 4, rw, 256), BF16),
        vm((g, 3, rw, 256), F32),
        vm((g, 3, rw, 256), F32),
        vm((g, 3, rw, 256), F32),
        vm((g, 3, rw, 256), F32),
        vm((4, 4 * nz, 128), F32),
        vm((16 * nz, 128), F32),
        vm((nz, 16, 128), BF16),
        vm((nz, 16, 128), BF16),
        vm((4, NT, 128), F32),
        vm((8 * nz, 128), F32),
        vm((nz, 8, 128), F32),
        vm((2, 8, 128), F32),
        vm((3, 2, 8, 128), F32),
        vm((8 * nz, 128), F32),
        vm((8, 128), F32),
        vm((7, 8, 128), F32),
    ]
    dma = pltpu.SemaphoreType.DMA
    scratch += [
        dma((6,)),
        dma((2,)),
        dma((2,)),
        dma((2, 4)),
        dma(()),
        dma((g,)),
        dma((2, g)),
        dma((2, g)),
        dma((2, g)),
        dma((2, g)),
        dma((2, g)),
        dma(()),
        dma(()),
        dma((2,)),
        dma((2,)),
        dma((2,)),
        dma((2,)),
    ]
    hbm = pl.BlockSpec(memory_space=pl.ANY)
    vmem = pl.BlockSpec(memory_space=pltpu.VMEM)
    return pl.pallas_call(
        kernel,
        out_shape=(
            jax.ShapeDtypeStruct((4, NT), F32),
            jax.ShapeDtypeStruct((NT, 512), F32),
        ),
        in_specs=[hbm, hbm, hbm, vmem],
        out_specs=(vmem, vmem),
        scratch_shapes=scratch,
        compiler_params=pltpu.CompilerParams(
            collective_id=0, has_side_effects=True, vmem_limit_bytes=48 * 1024 * 1024
        ),
    )(output_gradient, adapter_activations, proj, labels.reshape(1, 4))


def solution(mesh):
    placed = (P("dp", "param"), P("dp", None), P(("param", "dp"), None, None), P("dp"))
    return jax.shard_map(
        body,
        mesh=mesh,
        in_specs=placed,
        out_specs=(P("dp", None), P(None, "param")),
        check_vma=False,
    )
```

time: 1120 us -> 84.9 us (0.08)
  waiting for transfers between devices: 899 us -> 0 us
  blocking collectives: 186 us -> 0 us
  Pallas kernels: 0 us -> 76.3 us
  between operations: 14.5 us -> 0.66 us
    psum x1 -> x0, waiting for transfers between devices: 456 us -> none  [body(): totals, counts = lax.psum((totals, counts), 'dp')]
    unnamed x5 -> x0, waiting for transfers between devices: 444 us -> none
    psum x2 -> x0, blocking collectives: 143 us -> none  [the longest x1 128 us: body(): totals, counts = lax.psum((totals, counts), 'dp')]
    pallas_call x0 -> x1, Pallas kernels: none -> 76.3 us  [body(): pl.pallas_call(kernel, out_shape=(jax.ShapeDtypeStruct((4, NT), F32), jax...]
    all_to_all x1 -> x0, blocking collectives: 43.2 us -> none  [body(): lax.all_to_all(gradient, 'dp', split_axis=1, concat_axis=0, tiled=True)]
  transfers between devices with their start and end apart: 3 -> 0, of which waited for: 3 -> 0; matrix products, arithmetic and copies ran while one was open for 0% -> 0% of each run, Pallas kernels for 0% -> 0%
where the time goes in v1:
time: 84.9 us; the launch traced here: 83.3 us
  Pallas kernels  76.3 us (90%)
  local copies, waits for them, and re-layouts  6.35 us (7%)
    pallas_call x1, Pallas kernels, body(): pl.pallas_call(kernel, out_shape=(jax.ShapeDtypeStruct((4, NT), F32), jax...  76.3 us
    unnamed x9, local copies, waits for them, and re-layouts  6.35 us

profile of v1, /device:TPU:1, one launch (start us, length us, event | category | flops | bytes accessed | tf_op | source)
XLA Modules:
  0.0 83.3 jit_solution(3540819318746574979)
XLA Ops:
  0.6 1.1 %copy.6.act_h = bf16[1024,64]{1,0:T(8,128)(2,1)S(1)} copy(bf16[1024,64]{0,1:T(8,128)(2,1)} %param.5) | data formatting | bytes 262144 | tf_op args[1]
  1.7 0.0 copy-start
  1.7 2.2 %copy-done = bf16[8,64,4096]{2,1,0:T(8,128)(2,1)S(1)} copy-done((bf16[8,64,4096]{2,1,0:T(8,128)(2,1)S(1)}, bf16[8,64,4096]{2,1,0:T(8,128)(2,1)}, u32[]{:S(2)}) %copy-start) | copy-done | bytes 4194328
  3.9 0.0 copy-start.1
  3.9 1.2 %copy-done.1 = bf16[1024,512]{1,0:T(8,128)(2,1)S(1)} copy-done((bf16[1024,512]{1,0:T(8,128)(2,1)S(1)}, bf16[1024,512]{1,0:T(8,128)(2,1)}, u32[]{:S(2)}) %copy-start.1) | copy-done | bytes 1048600
  5.1 0.0 copy-start.2
  5.1 0.7 copy-done.2
  5.8 76.3 %shard_map.59 = (f32[4,32]{1,0:T(4,128)S(1)}, f32[32,512]{1,0:T(8,128)S(1)}) custom-call(bf16[1024,512]{1,0:T(8,128)(2,1)S(1)} %copy-done.1, bf16[1024,64]{1,0:T(8,128)(2,1)S(1)} %copy.6.act_h, bf16[512,4096]{1,0:T(8,128)(2,1)S(1)} %bitcast.2, s32[1,4]{1,0:T(1,128)S(1)} %bitcast.3), custom_call_target="tpu_custom_call" | custom-call | tf_op jit(solution)/shard_map/pallas_call | solution.py:398
  82.1 0.6 copy.9
  82.6 0.6 copy.10
Async XLA Ops:
  1.7 2.2 %copy-start = (bf16[8,64,4096]{2,1,0:T(8,128)(2,1)S(1)}, bf16[8,64,4096]{2,1,0:T(8,128)(2,1)}, u32[]{:S(2)}) copy-start(bf16[8,64,4096]{2,1,0:T(8,128)(2,1)} %param.6) | copy-start | bytes 12582916
  3.9 1.2 %copy-start.1 = (bf16[1024,512]{1,0:T(8,128)(2,1)S(1)}, bf16[1024,512]{1,0:T(8,128)(2,1)}, u32[]{:S(2)}) copy-start(bf16[1024,512]{1,0:T(8,128)(2,1)} %og_h.1) | copy-start | bytes 3145732
  5.1 0.7 copy-start.2

commit v2 on v0

v2 whole, which is shorter than its diff:
```python
import jax
import jax.numpy as jnp
from jax import lax
from jax.experimental import pallas as pl
from jax.experimental.pallas import tpu as pltpu
from jax.sharding import PartitionSpec as P

K = 4096
NT = 32
EPSILON = 1e-06
MESH = pl.DeviceIdType.MESH
F32 = jnp.float32
BF16 = jnp.bfloat16
HIGHEST = lax.Precision.HIGHEST

OFFSETS = (0, 1, 15, 2, 14, 3, 13, 4, 12, 5, 11, 6, 10, 7, 9, 8)
NZ = 16
GROUPS = 2
PER = NZ // GROUPS
RW = PER * 4


def flip(value, bits):
    for bit in (1, 2, 4):
        if bits & bit:
            value = value + bit - 2 * bit * ((value // bit) % 2)
    return value


def kernel(
    og_h, act_h, proj_h, lab_h, scores_ref, means_ref,
    og_v, act_v, proj_v, lab_v, g32, s32, qs, rb, f32s, ls, lr, lq, lqr,
    own, cs, cr, sx, rx, dsum, zs32, zs, zr, tpart, zts, ztr, agr, pks, pkr,
    in_sem, loc_sem, lab_sem, lq_sem, zg_send, zg_recv, core_sem, xy_sem,
    zs_sem, zt_sem, ag_sem, pk_sem,
):
    dp, param = lax.axis_index("dp"), lax.axis_index("param")
    z, q = dp // 4, dp % 4
    xl, y = param // 4, param % 4

    def ahead(i, s=0):
        return ((z + OFFSETS[i]) % NZ) * 4 + flip(q, s)

    def behind(i, s=0):
        return ((z + NZ - OFFSETS[i]) % NZ) * 4 + flip(q, s)

    def plane_peer(n):
        return (flip(dp, (n // 8) * 2), flip(param, n % 8))

    def remote(src, dst, send, recv, device):
        return pltpu.make_async_remote_copy(
            src_ref=src, dst_ref=dst, send_sem=send, recv_sem=recv,
            device_id=device, device_id_type=MESH,
        )

    def wait_all(ref, sem):
        pltpu.make_async_copy(ref, ref, sem).wait()

    barrier = pltpu.get_barrier_semaphore()
    peers = [(ahead(i, s), param) for i in reversed(range(NZ)) for s in range(4) if i or s]
    peers += [plane_peer(n) for n in range(1, 16) if n != 8]
    for peer in peers:
        pl.semaphore_signal(barrier, inc=1, device_id=peer, device_id_type=MESH)

    act_in = pltpu.make_async_copy(act_h, act_v, in_sem.at[0])
    act_in.start()
    lab_in = pltpu.make_async_copy(lab_h, lab_v, in_sem.at[6])
    lab_in.start()
    og_in = []
    for m in range(4):
        copy = pltpu.make_async_copy(
            og_h.at[pl.ds(m * 256, 256)], og_v.at[pl.ds(m * 256, 256)], in_sem.at[2 + m]
        )
        copy.start()
        og_in.append(copy)
    proj_in = pltpu.make_async_copy(proj_h, proj_v, in_sem.at[1])
    proj_in.start()

    act_in.wait()
    low = lax.broadcasted_iota(jnp.int32, (64, 128), 1) < 64
    for m in range(4):
        og_in[m].wait()
        act = act_v[:, m * 256 : (m + 1) * 256]
        g32[m] = lax.dot_general(
            og_v[m * 256 : (m + 1) * 256, :],
            jnp.concatenate([act, act], axis=0),
            (((0,), (1,)), ((), ())),
            preferred_element_type=F32,
        )
        for j in range(4):
            even = g32[m, pl.ds(2 * j, 64, stride=8), :]
            odd = g32[m, pl.ds(2 * j + 1, 64, stride=8), :]
            s32[pl.ds(m * 4 + j, 64, stride=16), :] = jnp.where(low, even, odd)
    for block in range(NZ):
        qs[block * 4 : block * 4 + 4] = (
            s32[block * 64 : (block + 1) * 64, :].astype(BF16).reshape(4, 16, 128)
        )
    lab_in.wait()
    lane = lax.broadcasted_iota(jnp.int32, (1, 128), 1)
    label_row = jnp.zeros((1, 128), jnp.int32)
    for m in range(4):
        label_row = jnp.where(lane % 4 == m, lab_v[0:1, m : m + 1], label_row)
    ls[...] = label_row

    pl.semaphore_wait(barrier, len(peers))

    for i in range(NZ):
        for s in range(4):
            if i or s:
                remote(
                    qs.at[ahead(i, s)], rb.at[i * 4 + s], zg_send, zg_recv.at[i // PER], (ahead(i, s), param)
                ).start()
        if i:
            remote(ls, lr.at[i], lab_sem.at[0], lab_sem.at[1], (ahead(i), param)).start()
    lr[0] = label_row
    home = pltpu.make_async_copy(qs.at[dp], rb.at[0], loc_sem)
    home.start()
    home.wait()
    proj_in.wait()

    def project(c):
        first = max(1, c * PER * 4)
        wait_all(rb.at[pl.ds(first, (c + 1) * PER * 4 - first)], zg_recv.at[c])
        for s in range(4):
            for k in range(PER):
                at = (s * PER + k) * 16
                f32s[c, at : at + 16, :] = rb[(c * PER + k) * 4 + s].astype(F32)
        rows = jnp.concatenate(
            [f32s[c, pl.ds(j, 4 * RW, stride=4), :].astype(BF16) for j in range(4)], axis=1
        )
        for n in range(8):
            part = jnp.dot(
                rows,
                proj_v[:, pl.ds(pl.multiple_of(flip(param, n) * 512, 512), 512)],
                preferred_element_type=F32,
            )
            for h in range(2):
                own[c, h * 8 + n] = part[2 * h * RW : (2 * h + 1) * RW]
                cs[c, h * 8 + n] = part[(2 * h + 1) * RW : (2 * h + 2) * RW].astype(BF16)
        remote(
            cs.at[c], cr.at[c], core_sem.at[0, c], core_sem.at[1, c], (flip(dp, 1), param)
        ).start()

    def after_core(c):
        wait_all(cr.at[c], core_sem.at[1, c])
        for n in range(16):
            total = own[c, n] + cr[c, n].astype(F32)
            if n:
                sx[c, n] = total.astype(BF16)
                remote(
                    sx.at[c, n], rx.at[c, n], xy_sem.at[0, c], xy_sem.at[1, c], plane_peer(n)
                ).start()
            else:
                own[c, 0] = total

    def after_plane(c):
        wait_all(rx.at[c, pl.ds(1, 15)], xy_sem.at[1, c])
        for j in range(4):
            columns = slice(j * 128, (j + 1) * 128)
            total = own[c, 0, :, columns]
            for n in range(1, 16):
                total += rx[c, n, :, columns].astype(F32)
            dsum[j, c * RW : (c + 1) * RW, :] = total

    def send_examples(c):
        base = c * PER * 16
        for j in range(4):
            for m in range(4):
                zs32[pl.ds(base + j * 4 + m, PER, stride=16), :] = dsum[
                    j, pl.ds(c * RW + m, PER, stride=4), :
                ]
        for k in range(PER):
            i = c * PER + k
            zs[i] = zs32[i * 16 : (i + 1) * 16, :].astype(BF16)
        for i in range(max(1, c * PER), (c + 1) * PER):
            remote(zs.at[i], zr.at[i], zs_sem.at[0], zs_sem.at[1], (behind(i), param)).start()

    for step in range(GROUPS + 2):
        if 0 <= step - 2 < GROUPS:
            after_plane(step - 2)
            if step - 2 < GROUPS - 1:
                send_examples(step - 2)
        if 0 <= step - 1 < GROUPS:
            after_core(step - 1)
            if step == GROUPS:
                wait_all(lr.at[pl.ds(1, NZ - 1)], lab_sem.at[1])
                labels = jnp.full((1, 128), -1, jnp.int32)
                for i in range(NZ):
                    labels = jnp.where(lane // 4 == i, lr[i], labels)
                lq[...] = labels
                for s in (1, 2, 3):
                    remote(lq, lqr.at[s - 1], lq_sem.at[0], lq_sem.at[1], (flip(dp, s), param)).start()
        if step < GROUPS:
            project(step)

    row = lax.broadcasted_iota(jnp.int32, (NT, 4 * NZ), 0)
    tag = row % 2
    for i in range(NZ):
        tag = jnp.where(row // 2 == i, row % 2 + 2 * (behind(i) // 4), tag)
    onehot = (tag == labels[:, : 4 * NZ]).astype(BF16)
    for j in range(4):
        values = dsum[j]
        high = values.astype(BF16)
        rest = (values - high.astype(F32)).astype(BF16)
        sums = jnp.dot(onehot, high, preferred_element_type=F32) + jnp.dot(
            onehot, rest, preferred_element_type=F32
        )
        for i in range(NZ):
            zts[i, j] = sums[2 * i : 2 * i + 2, :]
    for i in reversed(range(NZ)):
        for s in range(4):
            if i or s:
                remote(
                    zts.at[i, flip(q, s)], ztr.at[i * 4 + s], zt_sem.at[0], zt_sem.at[1], (behind(i, s), param)
                ).start()
    send_examples(GROUPS - 1)
    wait_all(ztr.at[pl.ds(1, 4 * NZ - 1)], zt_sem.at[1])
    agr[dp] = zts[0, q] + jnp.sum(ztr[1:], axis=0)
    for i in reversed(range(NZ)):
        for s in range(4):
            if i or s:
                remote(
                    agr.at[dp], agr.at[dp], ag_sem.at[0], ag_sem.at[1], (ahead(i, s), param)
                ).start()

    wait_all(zr.at[pl.ds(1, NZ - 1)], zs_sem.at[1])
    mine16 = zs32[0:16, :]
    for i in range(1, NZ):
        mine16 += zr[i].astype(F32)
    grad_sq = jnp.zeros((4, 128), F32)
    for j in range(4):
        grad_sq += mine16[j * 4 : (j + 1) * 4, :] * mine16[j * 4 : (j + 1) * 4, :]
    grad_sq = jnp.sum(grad_sq, axis=1, keepdims=True)
    wait_all(lqr, lq_sem.at[1])
    task = lax.broadcasted_iota(jnp.int32, (NT, 128), 0)
    counts = (task == labels).astype(F32)
    for s in range(3):
        counts += (task == lqr[s]).astype(F32)
    counts = jnp.maximum(jnp.sum(counts, axis=1, keepdims=True), 1.0)

    wait_all(agr.at[pl.ds(0, 4 * NZ - 1)], ag_sem.at[1])
    dots = jnp.zeros((4, NT), F32)
    mean_sq = jnp.zeros((4, NT), F32)
    ones = jnp.ones((4, 128), F32)
    contract = (((1,), (1,)), ((), ()))
    for j in range(4):
        for block in range(NZ):
            tpart[j, 2 * block : 2 * block + 2, :] = agr[block * 4 + j]
        means = tpart[j] / counts
        means_ref[:, j * 128 : (j + 1) * 128] = means
        part = mine16[j * 4 : (j + 1) * 4, :]
        dots += lax.dot_general(part, means, contract, precision=HIGHEST, preferred_element_type=F32)
        mean_sq += lax.dot_general(ones, means * means, contract, precision=HIGHEST, preferred_element_type=F32)
    pks[...] = jnp.zeros((8, 128), F32)
    pks[0:4, 0:NT] = dots
    pks[4:8, 0:NT] = mean_sq
    pks[0:4, 64:128] = jnp.broadcast_to(grad_sq, (4, 64))
    for n in range(1, 8):
        remote(pks, pkr.at[n - 1], pk_sem.at[0], pk_sem.at[1], (dp, flip(param, n))).start()
    wait_all(rb.at[pl.ds(1, 4 * NZ - 1)], zg_send)
    wait_all(lr.at[pl.ds(1, NZ - 1)], lab_sem.at[0])
    wait_all(lqr, lq_sem.at[0])
    for c in range(GROUPS):
        wait_all(cs.at[c], core_sem.at[0, c])
        wait_all(sx.at[c, pl.ds(1, 15)], xy_sem.at[0, c])
    wait_all(zs.at[pl.ds(1, NZ - 1)], zs_sem.at[0])
    wait_all(ztr.at[pl.ds(1, 4 * NZ - 1)], zt_sem.at[0])
    wait_all(agr.at[pl.ds(0, 4 * NZ - 1)], ag_sem.at[0])
    wait_all(pkr, pk_sem.at[1])
    total = pks[...]
    for n in range(7):
        total += pkr[n]
    scores_ref[...] = (
        total[0:4, 0:NT]
        / K
        * lax.rsqrt(total[0:4, 64 : 64 + NT] / K + EPSILON)
        * lax.rsqrt(total[4:8, 0:NT] / K + EPSILON)
    )
    wait_all(pkr, pk_sem.at[0])


def body(output_gradient, adapter_activations, proj, labels):
    proj = proj.reshape(proj.shape[0] * proj.shape[1], proj.shape[2])
    vm = pltpu.VMEM
    scratch = [
        vm((1024, 512), BF16),
        vm((64, 1024), BF16),
        vm((512, K), BF16),
        vm((1, 4), jnp.int32),
        vm((4, 512, 128), F32),
        vm((1024, 128), F32),
        vm((4 * NZ, 16, 128), BF16),
        vm((4 * NZ, 16, 128), BF16),
        vm((GROUPS, PER * 64, 128), F32),
        vm((1, 128), jnp.int32),
        vm((NZ, 1, 128), jnp.int32),
        vm((1, 128), jnp.int32),
        vm((3, 1, 128), jnp.int32),
        vm((GROUPS, 16, RW, 512), F32),
        vm((GROUPS, 16, RW, 512), BF16),
        vm((GROUPS, 16, RW, 512), BF16),
        vm((GROUPS, 16, RW, 512), BF16),
        vm((GROUPS, 16, RW, 512), BF16),
        vm((4, 4 * NZ, 128), F32),
        vm((16 * NZ, 128), F32),
        vm((NZ, 16, 128), BF16),
        vm((NZ, 16, 128), BF16),
        vm((4, NT, 128), F32),
        vm((NZ, 4, 2, 128), F32),
        vm((4 * NZ, 2, 128), F32),
        vm((4 * NZ, 2, 128), F32),
        vm((8, 128), F32),
        vm((7, 8, 128), F32),
    ]
    dma = pltpu.SemaphoreType.DMA
    scratch += [
        dma((7,)),
        dma(()),
        dma((2,)),
        dma((2,)),
        dma(()),
        dma((GROUPS,)),
        dma((2, GROUPS)),
        dma((2, GROUPS)),
        dma((2,)),
        dma((2,)),
        dma((2,)),
        dma((2,)),
    ]
    hbm = pl.BlockSpec(memory_space=pl.ANY)
    vmem = pl.BlockSpec(memory_space=pltpu.VMEM)
    return pl.pallas_call(
        kernel,
        out_shape=(
            jax.ShapeDtypeStruct((4, NT), F32),
            jax.ShapeDtypeStruct((NT, 512), F32),
        ),
        in_specs=[hbm, hbm, hbm, hbm],
        out_specs=(vmem, vmem),
        scratch_shapes=scratch,
        compiler_params=pltpu.CompilerParams(
            collective_id=0, has_side_effects=True, vmem_limit_bytes=63 * 1024 * 1024
        ),
    )(output_gradient, adapter_activations.T, proj, labels.reshape(1, 4))


def solution(mesh):
    placed = (P("dp", "param"), P("dp", None), P(("param", "dp"), None, None), P("dp"))
    return jax.shard_map(
        body,
        mesh=mesh,
        in_specs=placed,
        out_specs=(P("dp", None), P(None, "param")),
        check_vma=False,
    )
```

time: 1120 us -> 74.3 us (0.07)
  waiting for transfers between devices: 899 us -> 0 us
  blocking collectives: 186 us -> 0 us
  Pallas kernels: 0 us -> 70.8 us
  between operations: 14.5 us -> 0.64 us
    psum x1 -> x0, waiting for transfers between devices: 456 us -> none  [body(): totals, counts = lax.psum((totals, counts), 'dp')]
    unnamed x5 -> x0, waiting for transfers between devices: 444 us -> none
    psum x2 -> x0, blocking collectives: 143 us -> none  [the longest x1 128 us: body(): totals, counts = lax.psum((totals, counts), 'dp')]
    pallas_call x0 -> x1, Pallas kernels: none -> 70.8 us  [body(): pl.pallas_call(kernel, out_shape=(jax.ShapeDtypeStruct((4, NT), F32), jax...]
    all_to_all x1 -> x0, blocking collectives: 43.2 us -> none  [body(): lax.all_to_all(gradient, 'dp', split_axis=1, concat_axis=0, tiled=True)]
  transfers between devices with their start and end apart: 3 -> 0, of which waited for: 3 -> 0; matrix products, arithmetic and copies ran while one was open for 0% -> 0% of each run, Pallas kernels for 0% -> 0%
where the time goes in v2:
time: 74.3 us; the launch traced here: 74.1 us
  Pallas kernels  70.8 us (95%)
  local copies, waits for them, and re-layouts  2.72 us (4%)
    pallas_call x1, Pallas kernels, body(): pl.pallas_call(kernel, out_shape=(jax.ShapeDtypeStruct((4, NT), F32), jax...  70.8 us
    unnamed x2, local copies, waits for them, and re-layouts  2.72 us

profile of v2, /device:TPU:1, one launch (start us, length us, event | category | flops | bytes accessed | tf_op | source)
XLA Modules:
  0.0 74.1 jit_solution(17168873168068236402)
XLA Ops:
  0.6 70.8 %shard_map.59 = (f32[4,32]{1,0:T(4,128)}, f32[32,512]{1,0:T(8,128)}) custom-call(bf16[1024,512]{1,0:T(8,128)(2,1)} %og_h.1, bf16[64,1024]{1,0:T(8,128)(2,1)} %bitcast.4, bf16[512,4096]{1,0:T(8,128)(2,1)} %bitcast.3, s32[1,4]{1,0:T(1,128)} %bitcast.5), custom_call_target="tpu_custom_call" | custom-call | tf_op jit(solution)/shard_map/pallas_call | solution.py:332
  71.4 1.2 %copy.8 = f32[4,32]{1,0:T(4,128)} copy(f32[4,32]{1,0:T(4,128)} %get-tuple-element.4) | data formatting | bytes 1024
  72.7 1.5 %copy.9 = f32[32,512]{1,0:T(8,128)} copy(f32[32,512]{1,0:T(8,128)} %get-tuple-element.5) | data formatting | bytes 131072

commit v3 on v2

--- a/solution.py
+++ b/solution.py
@@ -30,9 +30,10 @@
 def kernel(
     og_h, act_h, proj_h, lab_h, scores_ref, means_ref,
     og_v, act_v, proj_v, lab_v, g32, s32, qs, rb, f32s, ls, lr, lq, lqr,
-    own, cs, cr, sx, rx, dsum, zs32, zs, zr, tpart, zts, ztr, agr, pks, pkr,
+    xs, own, cs, cr, sx, rx, dsum, zs32, zs, zr,
+    town, tcs, tcr, tsx, trx, ztb, ztr, agr, tpart, pks, pkr,
     in_sem, loc_sem, lab_sem, lq_sem, zg_send, zg_recv, core_sem, xy_sem,
-    zs_sem, zt_sem, ag_sem, pk_sem,
+    zs_sem, tc_sem, ty_sem, zt_sem, ag_sem, pk_sem,
 ):
     dp, param = lax.axis_index("dp"), lax.axis_index("param")
     z, q = dp // 4, dp % 4
@@ -55,12 +56,6 @@
 
     def wait_all(ref, sem):
         pltpu.make_async_copy(ref, ref, sem).wait()
-
-    barrier = pltpu.get_barrier_semaphore()
-    peers = [(ahead(i, s), param) for i in reversed(range(NZ)) for s in range(4) if i or s]
-    peers += [plane_peer(n) for n in range(1, 16) if n != 8]
-    for peer in peers:
-        pl.semaphore_signal(barrier, inc=1, device_id=peer, device_id_type=MESH)
 
     act_in = pltpu.make_async_copy(act_h, act_v, in_sem.at[0])
     act_in.start()
@@ -75,6 +70,17 @@
         og_in.append(copy)
     proj_in = pltpu.make_async_copy(proj_h, proj_v, in_sem.at[1])
     proj_in.start()
+
+    barrier = pltpu.get_barrier_semaphore()
+    far = [(ahead(i, s), param) for i in reversed(range(5, NZ)) for s in range(4)]
+    near = [(ahead(i, s), param) for i in reversed(range(5)) for s in range(4) if i or s]
+    near += [plane_peer(n) for n in range(1, 16) if n != 8]
+
+    def greet(peers):
+        for peer in peers:
+            pl.semaphore_signal(barrier, inc=1, device_id=peer, device_id_type=MESH)
+
+    greet(far)
 
     act_in.wait()
     low = lax.broadcasted_iota(jnp.int32, (64, 128), 1) < 64
@@ -91,6 +97,8 @@
             even = g32[m, pl.ds(2 * j, 64, stride=8), :]
             odd = g32[m, pl.ds(2 * j + 1, 64, stride=8), :]
             s32[pl.ds(m * 4 + j, 64, stride=16), :] = jnp.where(low, even, odd)
+        if m == 0:
+            greet(near)
     for block in range(NZ):
         qs[block * 4 : block * 4 + 4] = (
             s32[block * 64 : (block + 1) * 64, :].astype(BF16).reshape(4, 16, 128)
@@ -102,23 +110,23 @@
         label_row = jnp.where(lane % 4 == m, lab_v[0:1, m : m + 1], label_row)
     ls[...] = label_row
 
-    pl.semaphore_wait(barrier, len(peers))
-
+    pl.semaphore_wait(barrier, len(far) + len(near))
+
+    for i in range(1, NZ):
+        remote(ls, lr.at[i], lab_sem.at[0], lab_sem.at[1], (ahead(i), param)).start()
     for i in range(NZ):
         for s in range(4):
             if i or s:
                 remote(
                     qs.at[ahead(i, s)], rb.at[i * 4 + s], zg_send, zg_recv.at[i // PER], (ahead(i, s), param)
                 ).start()
-        if i:
-            remote(ls, lr.at[i], lab_sem.at[0], lab_sem.at[1], (ahead(i), param)).start()
     lr[0] = label_row
     home = pltpu.make_async_copy(qs.at[dp], rb.at[0], loc_sem)
     home.start()
     home.wait()
     proj_in.wait()
 
-    def project(c):
+    def arrange(c):
         first = max(1, c * PER * 4)
         wait_all(rb.at[pl.ds(first, (c + 1) * PER * 4 - first)], zg_recv.at[c])
         for s in range(4):
@@ -128,12 +136,16 @@
         rows = jnp.concatenate(
             [f32s[c, pl.ds(j, 4 * RW, stride=4), :].astype(BF16) for j in range(4)], axis=1
         )
+        xs[c] = rows
+
+    def projected(rows, n):
+        columns = pl.ds(pl.multiple_of(flip(param, n) * 512, 512), 512)
+        return jnp.dot(rows, proj_v[:, columns], preferred_element_type=F32)
+
+    def project(c):
+        rows = xs[c]
         for n in range(8):
-            part = jnp.dot(
-                rows,
-                proj_v[:, pl.ds(pl.multiple_of(flip(param, n) * 512, 512), 512)],
-                preferred_element_type=F32,
-            )
+            part = projected(rows, n)
             for h in range(2):
                 own[c, h * 8 + n] = part[2 * h * RW : (2 * h + 1) * RW]
                 cs[c, h * 8 + n] = part[(2 * h + 1) * RW : (2 * h + 2) * RW].astype(BF16)
@@ -175,47 +187,74 @@
         for i in range(max(1, c * PER), (c + 1) * PER):
             remote(zs.at[i], zr.at[i], zs_sem.at[0], zs_sem.at[1], (behind(i), param)).start()
 
-    for step in range(GROUPS + 2):
-        if 0 <= step - 2 < GROUPS:
-            after_plane(step - 2)
-            if step - 2 < GROUPS - 1:
-                send_examples(step - 2)
-        if 0 <= step - 1 < GROUPS:
-            after_core(step - 1)
-            if step == GROUPS:
-                wait_all(lr.at[pl.ds(1, NZ - 1)], lab_sem.at[1])
-                labels = jnp.full((1, 128), -1, jnp.int32)
-                for i in range(NZ):
-                    labels = jnp.where(lane // 4 == i, lr[i], labels)
-                lq[...] = labels
-                for s in (1, 2, 3):
-                    remote(lq, lqr.at[s - 1], lq_sem.at[0], lq_sem.at[1], (flip(dp, s), param)).start()
-        if step < GROUPS:
-            project(step)
-
+    for c in range(GROUPS - 1):
+        arrange(c)
+        project(c)
+        if c:
+            after_core(c - 1)
+
+    wait_all(lr.at[pl.ds(1, NZ - 1)], lab_sem.at[1])
+    labels = jnp.full((1, 128), -1, jnp.int32)
+    for i in range(NZ):
+        labels = jnp.where(lane // 4 == i, lr[i], labels)
+    lq[...] = labels
+    for s in (1, 2, 3):
+        remote(lq, lqr.at[s - 1], lq_sem.at[0], lq_sem.at[1], (flip(dp, s), param)).start()
+    if GROUPS > 1:
+        after_core(GROUPS - 2)
+    wait_all(lqr, lq_sem.at[1])
+
+    arrange(GROUPS - 1)
     row = lax.broadcasted_iota(jnp.int32, (NT, 4 * NZ), 0)
-    tag = row % 2
-    for i in range(NZ):
-        tag = jnp.where(row // 2 == i, row % 2 + 2 * (behind(i) // 4), tag)
-    onehot = (tag == labels[:, : 4 * NZ]).astype(BF16)
-    for j in range(4):
-        values = dsum[j]
-        high = values.astype(BF16)
-        rest = (values - high.astype(F32)).astype(BF16)
-        sums = jnp.dot(onehot, high, preferred_element_type=F32) + jnp.dot(
-            onehot, rest, preferred_element_type=F32
-        )
-        for i in range(NZ):
-            zts[i, j] = sums[2 * i : 2 * i + 2, :]
-    for i in reversed(range(NZ)):
-        for s in range(4):
-            if i or s:
-                remote(
-                    zts.at[i, flip(q, s)], ztr.at[i * 4 + s], zt_sem.at[0], zt_sem.at[1], (behind(i, s), param)
-                ).start()
+    tag = row % 8
+    for s in range(4):
+        tag = jnp.where(row // 8 == s, row % 8 + 8 * flip(q, s), tag)
+    sums = jnp.zeros((NT, 512), F32)
+    for s in range(4):
+        known = labels if s == 0 else lqr[s - 1]
+        onehot = (tag == known[:, : 4 * NZ]).astype(BF16)
+        rows = jnp.concatenate([xs[c, s * RW : (s + 1) * RW, :] for c in range(GROUPS)], axis=0)
+        sums += jnp.dot(onehot, rows, preferred_element_type=F32)
+    high = sums.astype(BF16)
+    parts = jnp.concatenate([high, (sums - high.astype(F32)).astype(BF16)], axis=0)
+    for n in range(8):
+        part = projected(parts, n)
+        part = part[:NT] + part[NT:]
+        for h in range(2):
+            town[h * 8 + n] = part[16 * h : 16 * h + 8]
+            tcs[h * 8 + n] = part[16 * h + 8 : 16 * h + 16]
+    remote(tcs, tcr, tc_sem.at[0], tc_sem.at[1], (flip(dp, 1), param)).start()
+    project(GROUPS - 1)
+
+    def stacked(value):
+        return jnp.concatenate([value[:, :256], value[:, 256:]], axis=0)
+
+    wait_all(tcr, tc_sem.at[1])
+    for n in range(1, 16):
+        tsx[n] = stacked(town[n] + tcr[n]).astype(BF16)
+        remote(tsx.at[n], trx.at[n], ty_sem.at[0], ty_sem.at[1], plane_peer(n)).start()
+    label_sums = stacked(town[0] + tcr[0])
+    after_core(GROUPS - 1)
+    for c in range(GROUPS - 1):
+        after_plane(c)
+        send_examples(c)
+
+    wait_all(trx.at[pl.ds(1, 15)], ty_sem.at[1])
+    for n in range(1, 16):
+        label_sums += trx[n].astype(F32)
+    for n in range(NZ):
+        ztb[n] = label_sums[n : n + 1, :]
+    for i in reversed(range(1, NZ)):
+        remote(
+            ztb.at[behind(i) // 4], ztr.at[i], zt_sem.at[0], zt_sem.at[1], (behind(i), param)
+        ).start()
+    after_plane(GROUPS - 1)
     send_examples(GROUPS - 1)
-    wait_all(ztr.at[pl.ds(1, 4 * NZ - 1)], zt_sem.at[1])
-    agr[dp] = zts[0, q] + jnp.sum(ztr[1:], axis=0)
+    wait_all(ztr.at[pl.ds(1, NZ - 1)], zt_sem.at[1])
+    total = ztb[z]
+    for i in range(1, NZ):
+        total += ztr[i]
+    agr[dp] = total
     for i in reversed(range(NZ)):
         for s in range(4):
             if i or s:
@@ -231,7 +270,6 @@
     for j in range(4):
         grad_sq += mine16[j * 4 : (j + 1) * 4, :] * mine16[j * 4 : (j + 1) * 4, :]
     grad_sq = jnp.sum(grad_sq, axis=1, keepdims=True)
-    wait_all(lqr, lq_sem.at[1])
     task = lax.broadcasted_iota(jnp.int32, (NT, 128), 0)
     counts = (task == labels).astype(F32)
     for s in range(3):
@@ -243,10 +281,11 @@
     mean_sq = jnp.zeros((4, NT), F32)
     ones = jnp.ones((4, 128), F32)
     contract = (((1,), (1,)), ((), ()))
+    for n in range(NZ):
+        for j in range(4):
+            tpart[n // 8, 8 * j + n % 8 : 8 * j + n % 8 + 1, :] = agr[n * 4 + j]
     for j in range(4):
-        for block in range(NZ):
-            tpart[j, 2 * block : 2 * block + 2, :] = agr[block * 4 + j]
-        means = tpart[j] / counts
+        means = tpart[j // 2, :, (j % 2) * 128 : (j % 2 + 1) * 128] / counts
         means_ref[:, j * 128 : (j + 1) * 128] = means
         part = mine16[j * 4 : (j + 1) * 4, :]
         dots += lax.dot_general(part, means, contract, precision=HIGHEST, preferred_element_type=F32)
@@ -264,7 +303,9 @@
         wait_all(cs.at[c], core_sem.at[0, c])
         wait_all(sx.at[c, pl.ds(1, 15)], xy_sem.at[0, c])
     wait_all(zs.at[pl.ds(1, NZ - 1)], zs_sem.at[0])
-    wait_all(ztr.at[pl.ds(1, 4 * NZ - 1)], zt_sem.at[0])
+    wait_all(tcs, tc_sem.at[0])
+    wait_all(tsx.at[pl.ds(1, 15)], ty_sem.at[0])
+    wait_all(ztr.at[pl.ds(1, NZ - 1)], zt_sem.at[0])
     wait_all(agr.at[pl.ds(0, 4 * NZ - 1)], ag_sem.at[0])
     wait_all(pkr, pk_sem.at[1])
     total = pks[...]
@@ -296,6 +337,7 @@
         vm((NZ, 1, 128), jnp.int32),
         vm((1, 128), jnp.int32),
         vm((3, 1, 128), jnp.int32),
+        vm((GROUPS, 4 * RW, 512), BF16),
         vm((GROUPS, 16, RW, 512), F32),
         vm((GROUPS, 16, RW, 512), BF16),
         vm((GROUPS, 16, RW, 512), BF16),
@@ -305,10 +347,15 @@
         vm((16 * NZ, 128), F32),
         vm((NZ, 16, 128), BF16),
         vm((NZ, 16, 128), BF16),
-        vm((4, NT, 128), F32),
-        vm((NZ, 4, 2, 128), F32),
-        vm((4 * NZ, 2, 128), F32),
-        vm((4 * NZ, 2, 128), F32),
+        vm((16, 8, 512), F32),
+        vm((16, 8, 512), F32),
+        vm((16, 8, 512), F32),
+        vm((16, 16, 256), BF16),
+        vm((16, 16, 256), BF16),
+        vm((NZ, 1, 256), F32),
+        vm((NZ, 1, 256), F32),
+        vm((4 * NZ, 1, 256), F32),
+        vm((2, NT, 256), F32),
         vm((8, 128), F32),
         vm((7, 8, 128), F32),
     ]
@@ -322,6 +369,8 @@
         dma((GROUPS,)),
         dma((2, GROUPS)),
         dma((2, GROUPS)),
+        dma((2,)),
+        dma((2,)),
         dma((2,)),
         dma((2,)),
         dma((2,)),

time: 74.3 us -> 68.4 us (0.921)
  Pallas kernels: 70.8 us -> 64.8 us
    pallas_call x1, Pallas kernels: 70.8 us -> 64.8 us  [body(): pl.pallas_call(kernel, out_shape=(jax.ShapeDtypeStruct((4, NT), F32), jax...]
where the time goes in v3:
time: 68.4 us; the launch traced here: 68.2 us
  Pallas kernels  64.8 us (95%)
  local copies, waits for them, and re-layouts  2.72 us (4%)
    pallas_call x1, Pallas kernels, body(): pl.pallas_call(kernel, out_shape=(jax.ShapeDtypeStruct((4, NT), F32), jax...  64.8 us
    unnamed x2, local copies, waits for them, and re-layouts  2.72 us

profile of v3, /device:TPU:1, one launch (start us, length us, event | category | flops | bytes accessed | tf_op | source)
XLA Modules:
  0.0 68.2 jit_solution(2758438941004644210)
XLA Ops:
  0.6 64.8 %shard_map.59 = (f32[4,32]{1,0:T(4,128)}, f32[32,512]{1,0:T(8,128)}) custom-call(bf16[1024,512]{1,0:T(8,128)(2,1)} %og_h.1, bf16[64,1024]{1,0:T(8,128)(2,1)} %bitcast.4, bf16[512,4096]{1,0:T(8,128)(2,1)} %bitcast.3, s32[1,4]{1,0:T(1,128)} %bitcast.5), custom_call_target="tpu_custom_call" | custom-call | tf_op jit(solution)/shard_map/pallas_call | solution.py:381
  65.4 1.2 %copy.8 = f32[4,32]{1,0:T(4,128)} copy(f32[4,32]{1,0:T(4,128)} %get-tuple-element.4) | data formatting | bytes 1024
  66.7 1.5 %copy.9 = f32[32,512]{1,0:T(8,128)} copy(f32[32,512]{1,0:T(8,128)} %get-tuple-element.5) | data formatting | bytes 131072

commit v4 on v3

--- a/solution.py
+++ b/solution.py
@@ -31,7 +31,7 @@
     og_h, act_h, proj_h, lab_h, scores_ref, means_ref,
     og_v, act_v, proj_v, lab_v, g32, s32, qs, rb, f32s, ls, lr, lq, lqr,
     xs, own, cs, cr, sx, rx, dsum, zs32, zs, zr,
-    town, tcs, tcr, tsx, trx, ztb, ztr, agr, tpart, pks, pkr,
+    town, tcs, tcr, tsx, trx, ztb, ztr, agr, pks, pkr,
     in_sem, loc_sem, lab_sem, lq_sem, zg_send, zg_recv, core_sem, xy_sem,
     zs_sem, tc_sem, ty_sem, zt_sem, ag_sem, pk_sem,
 ):
@@ -242,58 +242,41 @@
     wait_all(trx.at[pl.ds(1, 15)], ty_sem.at[1])
     for n in range(1, 16):
         label_sums += trx[n].astype(F32)
-    for n in range(NZ):
-        ztb[n] = label_sums[n : n + 1, :]
+    ztb[...] = label_sums.astype(BF16)
     for i in reversed(range(1, NZ)):
-        remote(
-            ztb.at[behind(i) // 4], ztr.at[i], zt_sem.at[0], zt_sem.at[1], (behind(i), param)
-        ).start()
+        remote(ztb, ztr.at[i], zt_sem.at[0], zt_sem.at[1], (ahead(i), param)).start()
     after_plane(GROUPS - 1)
     send_examples(GROUPS - 1)
     wait_all(ztr.at[pl.ds(1, NZ - 1)], zt_sem.at[1])
-    total = ztb[z]
     for i in range(1, NZ):
-        total += ztr[i]
-    agr[dp] = total
-    for i in reversed(range(NZ)):
-        for s in range(4):
-            if i or s:
-                remote(
-                    agr.at[dp], agr.at[dp], ag_sem.at[0], ag_sem.at[1], (ahead(i, s), param)
-                ).start()
+        label_sums += ztr[i].astype(F32)
+    agr[q] = jnp.concatenate([label_sums[:8], label_sums[8:]], axis=1)
+    for s in (2, 3, 1):
+        remote(agr.at[q], agr.at[q], ag_sem.at[0], ag_sem.at[1], (flip(dp, s), param)).start()
 
     wait_all(zr.at[pl.ds(1, NZ - 1)], zs_sem.at[1])
     mine16 = zs32[0:16, :]
     for i in range(1, NZ):
         mine16 += zr[i].astype(F32)
-    grad_sq = jnp.zeros((4, 128), F32)
-    for j in range(4):
-        grad_sq += mine16[j * 4 : (j + 1) * 4, :] * mine16[j * 4 : (j + 1) * 4, :]
-    grad_sq = jnp.sum(grad_sq, axis=1, keepdims=True)
+    mine = jnp.concatenate([mine16[j * 4 : (j + 1) * 4, :] for j in range(4)], axis=1)
+    mine = jnp.concatenate([mine, jnp.zeros((4, 512), F32)], axis=0)
+    grad_sq = jnp.sum(mine * mine, axis=1, keepdims=True)
     task = lax.broadcasted_iota(jnp.int32, (NT, 128), 0)
     counts = (task == labels).astype(F32)
     for s in range(3):
         counts += (task == lqr[s]).astype(F32)
     counts = jnp.maximum(jnp.sum(counts, axis=1, keepdims=True), 1.0)
 
-    wait_all(agr.at[pl.ds(0, 4 * NZ - 1)], ag_sem.at[1])
-    dots = jnp.zeros((4, NT), F32)
-    mean_sq = jnp.zeros((4, NT), F32)
-    ones = jnp.ones((4, 128), F32)
+    wait_all(agr.at[pl.ds(0, 3)], ag_sem.at[1])
+    means = agr[...].reshape(NT, 512) / counts
+    means_ref[...] = means
     contract = (((1,), (1,)), ((), ()))
-    for n in range(NZ):
-        for j in range(4):
-            tpart[n // 8, 8 * j + n % 8 : 8 * j + n % 8 + 1, :] = agr[n * 4 + j]
-    for j in range(4):
-        means = tpart[j // 2, :, (j % 2) * 128 : (j % 2 + 1) * 128] / counts
-        means_ref[:, j * 128 : (j + 1) * 128] = means
-        part = mine16[j * 4 : (j + 1) * 4, :]
-        dots += lax.dot_general(part, means, contract, precision=HIGHEST, preferred_element_type=F32)
-        mean_sq += lax.dot_general(ones, means * means, contract, precision=HIGHEST, preferred_element_type=F32)
-    pks[...] = jnp.zeros((8, 128), F32)
-    pks[0:4, 0:NT] = dots
-    pks[4:8, 0:NT] = mean_sq
-    pks[0:4, 64:128] = jnp.broadcast_to(grad_sq, (4, 64))
+    dots = lax.dot_general(mine, means, contract, precision=HIGHEST, preferred_element_type=F32)
+    mean_sq = lax.dot_general(
+        jnp.ones((8, 512), F32), means * means, contract, precision=HIGHEST, preferred_element_type=F32
+    )
+    pks[:, 0:64] = jnp.concatenate([dots, mean_sq], axis=1)
+    pks[:, 64:128] = jnp.broadcast_to(grad_sq, (8, 64))
     for n in range(1, 8):
         remote(pks, pkr.at[n - 1], pk_sem.at[0], pk_sem.at[1], (dp, flip(param, n))).start()
     wait_all(rb.at[pl.ds(1, 4 * NZ - 1)], zg_send)
@@ -306,7 +289,7 @@
     wait_all(tcs, tc_sem.at[0])
     wait_all(tsx.at[pl.ds(1, 15)], ty_sem.at[0])
     wait_all(ztr.at[pl.ds(1, NZ - 1)], zt_sem.at[0])
-    wait_all(agr.at[pl.ds(0, 4 * NZ - 1)], ag_sem.at[0])
+    wait_all(agr.at[pl.ds(0, 3)], ag_sem.at[0])
     wait_all(pkr, pk_sem.at[1])
     total = pks[...]
     for n in range(7):
@@ -315,7 +298,7 @@
         total[0:4, 0:NT]
         / K
         * lax.rsqrt(total[0:4, 64 : 64 + NT] / K + EPSILON)
-        * lax.rsqrt(total[4:8, 0:NT] / K + EPSILON)
+        * lax.rsqrt(total[0:4, NT : 2 * NT] / K + EPSILON)
     )
     wait_all(pkr, pk_sem.at[0])
 
@@ -352,10 +335,9 @@
         vm((16, 8, 512), F32),
         vm((16, 16, 256), BF16),
         vm((16, 16, 256), BF16),
-        vm((NZ, 1, 256), F32),
-        vm((NZ, 1, 256), F32),
-        vm((4 * NZ, 1, 256), F32),
-        vm((2, NT, 256), F32),
+        vm((16, 256), BF16),
+        vm((NZ, 16, 256), BF16),
+        vm((4, 8, 512), F32),
         vm((8, 128), F32),
         vm((7, 8, 128), F32),
     ]

time: 68.4 us -> 65.1 us (0.952); the launches traced: 68.2 us -> 63.8 us
  Pallas kernels: 64.8 us -> 60.5 us
    pallas_call x1, Pallas kernels: 64.8 us -> 60.5 us  [body(): pl.pallas_call(kernel, out_shape=(jax.ShapeDtypeStruct((4, NT), F32), jax...]
where the time goes in v4:
time: 65.1 us; the launch traced here: 63.8 us
  Pallas kernels  60.5 us (93%)
  local copies, waits for them, and re-layouts  2.72 us (4%)
    pallas_call x1, Pallas kernels, body(): pl.pallas_call(kernel, out_shape=(jax.ShapeDtypeStruct((4, NT), F32), jax...  60.5 us
    unnamed x2, local copies, waits for them, and re-layouts  2.72 us

profile of v4, /device:TPU:1, one launch (start us, length us, event | category | flops | bytes accessed | tf_op | source)
XLA Modules:
  0.0 63.8 jit_solution(5662863058791428137)
XLA Ops:
  0.6 60.5 %shard_map.59 = (f32[4,32]{1,0:T(4,128)}, f32[32,512]{1,0:T(8,128)}) custom-call(bf16[1024,512]{1,0:T(8,128)(2,1)} %og_h.1, bf16[64,1024]{1,0:T(8,128)(2,1)} %bitcast.4, bf16[512,4096]{1,0:T(8,128)(2,1)} %bitcast.3, s32[1,4]{1,0:T(1,128)} %bitcast.5), custom_call_target="tpu_custom_call" | custom-call | tf_op jit(solution)/shard_map/pallas_call | solution.py:363
  61.1 1.2 %copy.8 = f32[4,32]{1,0:T(4,128)} copy(f32[4,32]{1,0:T(4,128)} %get-tuple-element.4) | data formatting | bytes 1024
  62.4 1.5 %copy.9 = f32[32,512]{1,0:T(8,128)} copy(f32[32,512]{1,0:T(8,128)} %get-tuple-element.5) | data formatting | bytes 131072

commit v5 on v4

--- a/solution.py
+++ b/solution.py
@@ -370,7 +370,7 @@
         out_specs=(vmem, vmem),
         scratch_shapes=scratch,
         compiler_params=pltpu.CompilerParams(
-            collective_id=0, has_side_effects=True, vmem_limit_bytes=63 * 1024 * 1024
+            collective_id=0, has_side_effects=True, vmem_limit_bytes=55040 * 1024
         ),
     )(output_gradient, adapter_activations.T, proj, labels.reshape(1, 4))
 

time: 65.1 us -> 63.5 us (0.975); the launches traced: 63.8 us -> 62.9 us
  local copies, waits for them, and re-layouts: 2.72 us -> 1.86 us
    unnamed x2 -> x4, local copies, waits for them, and re-layouts: 2.72 us -> 1.86 us
where the time goes in v5:
time: 63.5 us; the launch traced here: 62.9 us
  Pallas kernels  60.4 us (95%)
  local copies, waits for them, and re-layouts  1.86 us (3%)
  between operations  0.65 us (1%)
    pallas_call x1, Pallas kernels, body(): pl.pallas_call(kernel, out_shape=(jax.ShapeDtypeStruct((4, NT), F32), jax...  60.4 us
    unnamed x4, local copies, waits for them, and re-layouts  1.86 us

profile of v5, /device:TPU:1, one launch (start us, length us, event | category | flops | bytes accessed | tf_op | source)
XLA Modules:
  0.0 62.9 jit_solution(10136837457469344443)
XLA Ops:
  0.6 0.0 copy-start
  0.6 0.6 %copy-done = s32[4]{0:T(128)S(1)} copy-done((s32[4]{0:T(128)S(1)}, s32[4]{0:T(128)}, u32[]{:S(2)}) %copy-start) | copy-done | bytes 40
  1.3 60.4 %shard_map.59 = (f32[4,32]{1,0:T(4,128)S(1)}, f32[32,512]{1,0:T(8,128)S(1)}) custom-call(bf16[1024,512]{1,0:T(8,128)(2,1)} %og_h.1, bf16[64,1024]{1,0:T(8,128)(2,1)} %bitcast.5, bf16[512,4096]{1,0:T(8,128)(2,1)} %bitcast.4, s32[1,4]{1,0:T(1,128)S(1)} %bitcast.3), custom_call_target="tpu_custom_call" | custom-call | tf_op jit(solution)/shard_map/pallas_call | solution.py:363
  61.7 0.6 copy.8
  62.3 0.6 copy.9
Async XLA Ops:
  0.6 0.7 %copy-start = (s32[4]{0:T(128)S(1)}, s32[4]{0:T(128)}, u32[]{:S(2)}) copy-start(s32[4]{0:T(128)} %param.7) | copy-start | bytes 52

commit v6 on v5

--- a/solution.py
+++ b/solution.py
@@ -72,8 +72,8 @@
     proj_in.start()
 
     barrier = pltpu.get_barrier_semaphore()
-    far = [(ahead(i, s), param) for i in reversed(range(5, NZ)) for s in range(4)]
-    near = [(ahead(i, s), param) for i in reversed(range(5)) for s in range(4) if i or s]
+    far = [(ahead(i, s), param) for i in reversed(range(9, NZ)) for s in range(4)]
+    near = [(ahead(i, s), param) for i in reversed(range(9)) for s in range(4) if i or s]
     near += [plane_peer(n) for n in range(1, 16) if n != 8]
 
     def greet(peers):

time: 63.5 us -> 63.1 us (level)
  no operation moved by 1% of the time
where the time goes in v6:
time: 63.1 us; the launch traced here: 62.7 us
  Pallas kernels  60.2 us (95%)
  local copies, waits for them, and re-layouts  1.86 us (3%)
  between operations  0.65 us (1%)
    pallas_call x1, Pallas kernels, body(): pl.pallas_call(kernel, out_shape=(jax.ShapeDtypeStruct((4, NT), F32), jax...  60.2 us
    unnamed x4, local copies, waits for them, and re-layouts  1.86 us

profile of v6, /device:TPU:1, one launch (start us, length us, event | category | flops | bytes accessed | tf_op | source)
XLA Modules:
  0.0 62.7 jit_solution(2633029736940022444)
XLA Ops:
  0.6 0.0 copy-start
  0.6 0.6 %copy-done = s32[4]{0:T(128)S(1)} copy-done((s32[4]{0:T(128)S(1)}, s32[4]{0:T(128)}, u32[]{:S(2)}) %copy-start) | copy-done | bytes 40
  1.3 60.2 %shard_map.59 = (f32[4,32]{1,0:T(4,128)S(1)}, f32[32,512]{1,0:T(8,128)S(1)}) custom-call(bf16[1024,512]{1,0:T(8,128)(2,1)} %og_h.1, bf16[64,1024]{1,0:T(8,128)(2,1)} %bitcast.5, bf16[512,4096]{1,0:T(8,128)(2,1)} %bitcast.4, s32[1,4]{1,0:T(1,128)S(1)} %bitcast.3), custom_call_target="tpu_custom_call" | custom-call | tf_op jit(solution)/shard_map/pallas_call | solution.py:363
  61.5 0.6 copy.8
  62.0 0.6 %copy.9 = f32[32,512]{1,0:T(8,128)} copy(f32[32,512]{1,0:T(8,128)S(1)} %get-tuple-element.5) | data formatting | bytes 131072
Async XLA Ops:
  0.6 0.7 %copy-start = (s32[4]{0:T(128)S(1)}, s32[4]{0:T(128)}, u32[]{:S(2)}) copy-start(s32[4]{0:T(128)} %param.7) | copy-start | bytes 52

commit v7 on v6

--- a/solution.py
+++ b/solution.py
@@ -272,9 +272,12 @@
     means_ref[...] = means
     contract = (((1,), (1,)), ((), ()))
     dots = lax.dot_general(mine, means, contract, precision=HIGHEST, preferred_element_type=F32)
-    mean_sq = lax.dot_general(
-        jnp.ones((8, 512), F32), means * means, contract, precision=HIGHEST, preferred_element_type=F32
-    )
+    squares = means * means
+    high = squares.astype(BF16)
+    ones = jnp.ones((8, 512), BF16)
+    mean_sq = lax.dot_general(ones, high, contract, preferred_element_type=F32)
+    rest = (squares - high.astype(F32)).astype(BF16)
+    mean_sq += lax.dot_general(ones, rest, contract, preferred_element_type=F32)
     pks[:, 0:64] = jnp.concatenate([dots, mean_sq], axis=1)
     pks[:, 64:128] = jnp.broadcast_to(grad_sq, (8, 64))
     for n in range(1, 8):

time: 63.1 us -> 63 us (level)
  no operation moved by 1% of the time
where the time goes in v7:
time: 63 us; the launch traced here: 62.9 us
  Pallas kernels  60.4 us (96%)
  local copies, waits for them, and re-layouts  1.86 us (3%)
  between operations  0.65 us (1%)
    pallas_call x1, Pallas kernels, body(): pl.pallas_call(kernel, out_shape=(jax.ShapeDtypeStruct((4, NT), F32), jax...  60.4 us
    unnamed x4, local copies, waits for them, and re-layouts  1.86 us

profile of v7, /device:TPU:1, one launch (start us, length us, event | category | flops | bytes accessed | tf_op | source)
XLA Modules:
  0.0 62.9 jit_solution(14540937573109471014)
XLA Ops:
  0.6 0.0 copy-start
  0.6 0.6 %copy-done = s32[4]{0:T(128)S(1)} copy-done((s32[4]{0:T(128)S(1)}, s32[4]{0:T(128)}, u32[]{:S(2)}) %copy-start) | copy-done | bytes 40
  1.3 60.4 %shard_map.59 = (f32[4,32]{1,0:T(4,128)S(1)}, f32[32,512]{1,0:T(8,128)S(1)}) custom-call(bf16[1024,512]{1,0:T(8,128)(2,1)} %og_h.1, bf16[64,1024]{1,0:T(8,128)(2,1)} %bitcast.5, bf16[512,4096]{1,0:T(8,128)(2,1)} %bitcast.4, s32[1,4]{1,0:T(1,128)S(1)} %bitcast.3), custom_call_target="tpu_custom_call" | custom-call | tf_op jit(solution)/shard_map/pallas_call | solution.py:366
  61.7 0.6 copy.8
  62.2 0.6 %copy.9 = f32[32,512]{1,0:T(8,128)} copy(f32[32,512]{1,0:T(8,128)S(1)} %get-tuple-element.5) | data formatting | bytes 131072
Async XLA Ops:
  0.6 0.7 %copy-start = (s32[4]{0:T(128)S(1)}, s32[4]{0:T(128)}, u32[]{:S(2)}) copy-start(s32[4]{0:T(128)} %param.7) | copy-start | bytes 52
